TPU v7x, 32 devices: a whole 2x2x4 slice. The times are simulated.
32 devices in a mesh: area: 8 (over z, y), blk: 4 (over x, core).
Axes of the slice: x: 2, y: 2, z: 4, core: 2. Of those that a mesh axis runs over, the one named last changes fastest.
Arguments:
- activity: float32 [64, 4, 64, 128], P('area', 'blk'), may hold values from -8 to 8
- ext_input: bfloat16 [64, 4, 64, 128], P('area', 'blk'), may hold values from -5 to 5
- weights: bfloat16 [24, 4, 128, 512], P('area', 'blk'), may hold values from -0.25 to 0.25
- slot_dst: int32 [24], P('area'), may hold values from 0 to 7
- slot_src: int32 [24], P('area'), may hold values from 0 to 63, as said below
- slot_count: int32 [8], P('area'), may hold values from 3 to 3, as said below
- hebb_mask: int32 [24], P('area'), may hold values 0 or 1
Outputs:
- final_activity: float32 [64, 4, 64, 128], P('area', 'blk')
- plasticity: bfloat16 [24, 4, 128, 512], P('area', 'blk')
Inputs may be any that keep to these rules, and one draw needn't show every extreme that they name: Index i of area holds area i // 4; sources lie in areas listed for it by a connectome over the areas that always lists the area itself, the areas beside it on both sides (counted round) and the opposite one. Slots 0, 1 and 2 of index i of area have their source sub-blocks held by indices (i - 1) mod 8, (i + 1) mod 8 and (i + 4) mod 8. Among the occupied slots of one index of area, at most 1 have source sub-blocks held by one index of area (slot_src // 8); some index of area reaches 1. `slot_count`: some index of area has all 3 slots occupied.
All inputs are finite; a program needn't handle non-finite values. No bound on the sum of `hebb_mask` on one device may be relied on, other than what follows from the above.
Results may differ from a plain program's by a relative error of at most 0.014.
Values may be sent and summed in bfloat16 or wider, within the bound.
A program may use at most 64 MiB of HBM per device.

v0:
```python
import jax
import jax.numpy as jnp
from jax import lax
from jax.sharding import PartitionSpec as P

STEPS = 4


euler_step = 0.5


def request_rosters(src_rows, count_now, sub_dev, n_areas, link_cap):
    slot_cap = src_rows.shape[0]
    slot_ids = jnp.arange(slot_cap)
    occupied = slot_ids < count_now
    owner_idx = src_rows // sub_dev
    local_idx = src_rows % sub_dev
    earlier = (
        (owner_idx[:, None] == owner_idx[None, :])
        & occupied[None, :]
        & (slot_ids[None, :] < slot_ids[:, None])
    )
    link_idx = jnp.minimum(jnp.sum(earlier.astype(jnp.int32), axis=1), link_cap - 1)
    matches = (
        occupied[:, None, None]
        & (owner_idx[:, None, None] == jnp.arange(n_areas)[None, :, None])
        & (link_idx[:, None, None] == jnp.arange(link_cap)[None, None, :])
    )
    request_table = jnp.sum(jnp.where(matches, (local_idx + 1)[:, None, None], 0), axis=0)
    return (occupied, owner_idx, link_idx, request_table)


def body(activity, ext_input, weights, slot_dst, slot_src, slot_count, hebb_mask):
    n_areas = lax.axis_size("area")
    my_blk = lax.axis_index("blk")
    sub_dev = activity.shape[0]
    trials = activity.shape[2]
    quarter = activity.shape[3]
    slot_cap = slot_src.shape[0]
    sub_width = weights.shape[3]
    link_cap = (slot_cap + n_areas - 1) // n_areas
    occupied, owner_idx, link_idx, request_table = request_rosters(
        slot_src, slot_count[0], sub_dev, n_areas, link_cap
    )
    needed_rows = lax.all_to_all(request_table, "area", split_axis=0, concat_axis=0, tiled=True)
    is_valid = needed_rows > 0
    pick_idx = jnp.maximum(needed_rows - 1, 0)
    select = ((slot_dst[:, None] == jnp.arange(sub_dev)[None, :]) & occupied[:, None]).astype(
        jnp.float32
    )
    slot_weights = weights[:, 0]
    pre_list = []
    post_list = []
    full_act, full_ext = (
        lax.all_gather(activity.astype(jnp.bfloat16), "blk", axis=1, tiled=True).astype(
            activity.dtype
        ),
        lax.all_gather(
            ext_input.astype(jnp.float32).astype(jnp.bfloat16), "blk", axis=1, tiled=True
        ).astype(jnp.float32),
    )
    current = full_act.transpose(0, 2, 1, 3).reshape(sub_dev, trials, sub_width)
    drive_in = full_ext.transpose(0, 2, 1, 3).reshape(sub_dev, trials, sub_width)
    rate_full = jnp.tanh(current).astype(jnp.bfloat16)
    for step_idx in range(STEPS):
        rates_own = lax.dynamic_slice_in_dim(rate_full, my_blk * quarter, quarter, 2)
        outbound_rates = jnp.where(
            is_valid[:, :, None, None], rates_own[pick_idx], jnp.zeros((), jnp.bfloat16)
        )
        presynaptic_rates = lax.all_to_all(
            outbound_rates, "area", split_axis=0, concat_axis=0, tiled=True
        )[owner_idx, link_idx]
        input_contribution = jnp.einsum(
            "xvy,xye->xve", presynaptic_rates, slot_weights, preferred_element_type=jnp.float32
        )
        partial_value = jnp.einsum(
            "kd,kts->dts", select, input_contribution, precision=lax.Precision.HIGHEST
        )
        partial_value, presynaptic_rates = (partial_value, presynaptic_rates)
        summed = lax.psum(partial_value.astype(jnp.bfloat16), "blk").astype(jnp.float32)
        current = current + euler_step * (summed - current + drive_in)
        rate_full = jnp.tanh(current).astype(jnp.bfloat16)
        pre_list.append(presynaptic_rates)
        post_list.append(rate_full)
    final_state = lax.dynamic_slice_in_dim(current, my_blk * quarter, quarter, 2)[:, None]
    pre_all = jnp.stack(pre_list, axis=1).astype(jnp.float32)
    pre_centered = (pre_all - jnp.mean(pre_all, axis=2, keepdims=True)).astype(jnp.bfloat16)
    pre_centered = pre_centered.reshape(slot_cap, STEPS * trials, quarter)
    post_all = jnp.stack(post_list, axis=1).astype(jnp.float32)
    post_centered = (post_all - jnp.mean(post_all, axis=2, keepdims=True)).astype(jnp.bfloat16)
    post_slot = post_centered[slot_dst].reshape(slot_cap, STEPS * trials, sub_width)
    change = jnp.einsum("knq,kns->kqs", pre_centered, post_slot, preferred_element_type=jnp.float32)
    gate_on = (occupied & (hebb_mask == 1)).astype(jnp.float32)
    norm_scale = (STEPS * trials) ** (-0.5)
    plasticity = (change * gate_on[:, None, None] * norm_scale).astype(jnp.bfloat16)[:, None]
    return (final_state, plasticity)


def solution(mesh):
    in_specs = (
        P("area", "blk", None, None),
        P("area", "blk", None, None),
        P("area", "blk", None, None),
        P("area"),
        P("area"),
        P("area"),
        P("area"),
    )
    out_specs = (P("area", "blk", None, None), P("area", "blk", None, None))
    return jax.shard_map(body, mesh=mesh, in_specs=in_specs, out_specs=out_specs, check_vma=False)
```

profile of v0, /device:TPU:0, one launch (start us, length us, event | category | flops | bytes accessed | tf_op | source)
XLA Modules:
  0.0 250.6 jit_solution(7100204299055840622)
XLA Ops:
  8.5 1.2 and_convert_fusion
  10.7 7.3 %all-to-all-start = ((s32[8,1,1]{2,1,0:T(1,128)}), s32[8,1,1]{2,1,0:T(1,128)S(1)}, u32[]{:S(2)}, u32[]{:S(2)}) async-start(s32[8,1,1]{2,1,0:T(1,128)} %copy.91), calls=%async_computation | async-start | bytes 8192 | tf_op jit(solution)/shard_map/all_to_all | solution.py:45
  18.0 1.0 convert_element_type.74
  19.0 7.2 %all_gather.6 = bf16[8,4,64,128]{3,2,1,0:T(8,128)(2,1)S(1)} all-gather(bf16[8,1,64,128]{3,2,1,0:T(8,128)(2,1)S(1)} %convert_element_type.74), channel_id=1, replica_groups=mesh['area'=8,'blk'=4] {'blk'}, dimensions={1}, use_global_device_ids=true | all-gather | bytes 655360 | tf_op jit(solution)/shard_map/all_gather | solution.py:55
  28.8 6.0 %all-to-all-start.1 = ((bf16[8,1,64,128]{3,2,1,0:T(8,128)(2,1)}), bf16[8,1,64,128]{3,2,1,0:T(8,128)(2,1)S(1)}, u32[]{:S(2)}, u32[]{:S(2)}) async-start(bf16[8,1,64,128]{3,2,1,0:T(8,128)(2,1)} %fusion.30), calls=%async_computation.1 | async-start | bytes 262144 | tf_op jit(solution)/shard_map/all_to_all | solution.py:70
  34.9 7.0 %all_gather.7 = bf16[8,4,64,128]{3,2,1,0:T(8,128)(2,1)S(1)} all-gather(bf16[8,1,64,128]{3,2,1,0:T(8,128)(2,1)S(1)} %copy-done.9), channel_id=1, replica_groups=mesh['area'=8,'blk'=4] {'blk'}, dimensions={1}, use_global_device_ids=true | all-gather | bytes 655360 | tf_op jit(solution)/shard_map/all_gather | solution.py:58
  43.1 1.7 convolution_convert_fusion.3
  45.0 33.4 %all-reduce.5.cloned.1.call-done = bf16[8,64,512]{2,0,1:T(8,128)(2,1)} async-done(((bf16[8,64,512]{2,0,1:T(8,128)(2,1)}), bf16[8,64,512]{2,0,1:T(8,128)(2,1)}) %all-reduce.5.cloned.1.call-update) | async-done | bytes 524304 | tf_op jit(solution)/shard_map/psum | solution.py:80
  78.4 2.2 tanh_convert_fusion.3
  82.2 12.7 %all_to_all.29 = bf16[8,1,64,128]{3,2,1,0:T(8,128)(2,1)S(1)} all-to-all(bf16[8,1,64,128]{3,2,1,0:T(8,128)(2,1)S(1)} %fusion.29), channel_id=1, replica_groups=mesh['area'=8,'blk'=4] {'area'}, dimensions={0} | all-to-all | bytes 262144 | tf_op jit(solution)/shard_map/all_to_all | solution.py:70
  95.6 1.7 convolution_convert_fusion.2
  97.3 30.1 %all-reduce.7.cloned.1.call-done = bf16[8,64,512]{2,0,1:T(8,128)(2,1)} async-done(((bf16[8,64,512]{2,0,1:T(8,128)(2,1)}), bf16[8,64,512]{2,0,1:T(8,128)(2,1)}) %all-reduce.7.cloned.1.call-update) | async-done | bytes 524304 | tf_op jit(solution)/shard_map/psum | solution.py:80
  127.5 2.3 tanh_convert_fusion.2
  130.4 2.1 gather_fusion.4
  132.6 1.0 fusion.28
  133.6 12.8 %all_to_all.30 = bf16[8,1,64,128]{3,2,1,0:T(8,128)(2,1)} all-to-all(bf16[8,1,64,128]{3,2,1,0:T(8,128)(2,1)S(1)} %fusion.28), channel_id=1, replica_groups=mesh['area'=8,'blk'=4] {'area'}, dimensions={0} | all-to-all | bytes 262144 | tf_op jit(solution)/shard_map/all_to_all | solution.py:70
  146.3 2.1 gather_fusion.5
  148.4 1.0 fusion.20
  149.4 1.7 convolution_convert_fusion.1
  151.1 30.2 %all-reduce.9.cloned.1.call-done = bf16[8,64,512]{2,0,1:T(8,128)(2,1)} async-done(((bf16[8,64,512]{2,0,1:T(8,128)(2,1)}), bf16[8,64,512]{2,0,1:T(8,128)(2,1)}) %all-reduce.9.cloned.1.call-update) | async-done | bytes 524304 | tf_op jit(solution)/shard_map/psum | solution.py:80
  181.3 2.6 %tanh_convert_fusion.1 = bf16[8,64,512]{2,0,1:T(8,128)(2,1)S(1)} fusion(f32[8,64,4,128]{3,1,2,0:T(8,128)S(1)} %convert_bitcast_fusion, bf16[8,64,512]{2,0,1:T(8,128)(2,1)} %all-reduce.9.cloned.1.call-done, bf16[8,64,512]{2,0,1:T(8,128)(2,1)} %all-reduce.7.cloned.1.call-done, bf16[8,64,512]{2,0,1:T(8,128)(2,1)S(1)} %copy-done.1, ...), kind=kLoop, calls=%fused_computation.37 | loop fusion | flops 4194304 | bytes 4194304 | tf_op jit(solution)/shard_map/convert_element_type | solution.py:82
  185.4 2.1 gather_fusion.6
  187.5 1.6 fusion.27
  189.2 5.5 %all-to-all-start.4 = ((bf16[8,1,64,128]{3,2,1,0:T(8,128)(2,1)}), bf16[8,1,64,128]{3,2,1,0:T(8,128)(2,1)}, u32[]{:S(2)}, u32[]{:S(2)}) async-start(bf16[8,1,64,128]{3,2,1,0:T(8,128)(2,1)} %fusion.27), calls=%async_computation.4 | async-start | bytes 262144 | tf_op jit(solution)/shard_map/all_to_all | solution.py:70
  195.6 6.6 %all-to-all-done.4 = bf16[8,1,64,128]{3,2,1,0:T(8,128)(2,1)} async-done(((bf16[8,1,64,128]{3,2,1,0:T(8,128)(2,1)}), bf16[8,1,64,128]{3,2,1,0:T(8,128)(2,1)}, u32[]{:S(2)}, u32[]{:S(2)}) %all-to-all-start.4) | async-done | bytes 131104 | tf_op jit(solution)/shard_map/all_to_all | solution.py:70
  202.1 2.1 gather_fusion.7
  204.2 1.0 fusion.18
  205.2 1.7 convolution_convert_fusion
  207.9 0.9 fusion.17
  209.5 27.6 %all-reduce.11.cloned.1.call-done = bf16[8,64,512]{2,0,1:T(8,128)(2,1)} async-done(((bf16[8,64,512]{2,0,1:T(8,128)(2,1)}), bf16[8,64,512]{2,0,1:T(8,128)(2,1)}) %all-reduce.11.cloned.1.call-update) | async-done | bytes 524304 | tf_op jit(solution)/shard_map/psum | solution.py:80
  237.1 2.9 %fusion.12 = (bf16[8,1,64,512]{3,0,2,1:T(8,128)(2,1)S(1)}, f32[8,64,512]{2,0,1:T(8,128)S(1)}) fusion(bf16[8,64,512]{2,0,1:T(8,128)(2,1)} %all-reduce.11.cloned.1.call-done, bf16[8,64,512]{2,0,1:T(8,128)(2,1)} %all-reduce.9.cloned.1.call-done, bf16[8,64,512]{2,0,1:T(8,128)(2,1)} %all-reduce.7.cloned.1.call-done, ...), kind=kLoop, calls=%fused_computation.40 | loop fusion | flops 5505024 | bytes 5767168 | tf_op jit(solution)/shard_map/stack | solution.py:89
  243.0 1.1 fusion.3
  (75 shorter events, 15.6 us)
Async XLA Ops:
  7.2 35.7 %copy-start = (bf16[3,1,128,512]{3,2,1,0:T(8,128)(2,1)S(1)}, bf16[3,1,128,512]{3,2,1,0:T(8,128)(2,1)}, u32[]{:S(2)}) copy-start(bf16[3,1,128,512]{3,2,1,0:T(8,128)(2,1)} %param.9) | copy-start | bytes 1179652
  10.7 16.3 %all-to-all-start = ((s32[8,1,1]{2,1,0:T(1,128)}), s32[8,1,1]{2,1,0:T(1,128)S(1)}, u32[]{:S(2)}, u32[]{:S(2)}) async-start(s32[8,1,1]{2,1,0:T(1,128)} %copy.91), calls=%async_computation | async-start | bytes 8192 | tf_op jit(solution)/shard_map/all_to_all | solution.py:45
  26.3 8.6 %copy-start.9 = (bf16[8,1,64,128]{3,2,1,0:T(8,128)(2,1)S(1)}, bf16[8,1,64,128]{3,2,1,0:T(8,128)(2,1)}, u32[]{:S(2)}) copy-start(bf16[8,1,64,128]{3,2,1,0:T(8,128)(2,1)} %param.8) | copy-start | bytes 393220
  26.3 15.6 %copy-start.11 = (s32[3]{0:T(128)S(1)}, s32[3]{0:T(128)}, u32[]{:S(2)}) copy-start(s32[3]{0:T(128)} %param.10) | copy-start | bytes 40
  28.8 13.5 %all-to-all-start.1 = ((bf16[8,1,64,128]{3,2,1,0:T(8,128)(2,1)}), bf16[8,1,64,128]{3,2,1,0:T(8,128)(2,1)S(1)}, u32[]{:S(2)}, u32[]{:S(2)}) async-start(bf16[8,1,64,128]{3,2,1,0:T(8,128)(2,1)} %fusion.30), calls=%async_computation.1 | async-start | bytes 262144 | tf_op jit(solution)/shard_map/all_to_all | solution.py:70
  34.8 43.6 %all-reduce.5.cloned.1.call-start = ((), (), s32[]{:S(2)}) async-start(), calls=%async_computation.5 | async-start | bytes 1048576 | tf_op jit(solution)/shard_map/psum | solution.py:80
  42.9 1.9 copy-start.7
  44.8 82.6 %all-reduce.7.cloned.1.call-start = ((), (), s32[]{:S(2)}) async-start(), calls=%async_computation.6 | async-start | bytes 1048576 | tf_op jit(solution)/shard_map/psum | solution.py:80
  80.6 0.8 copy-start.2
  81.4 46.0 %copy-start.1 = (bf16[8,64,512]{2,0,1:T(8,128)(2,1)S(1)}, bf16[8,64,512]{2,0,1:T(8,128)(2,1)}, u32[]{:S(2)}) copy-start(bf16[8,64,512]{2,0,1:T(8,128)(2,1)} %all-reduce.5.cloned.1.call-done) | copy-start | bytes 1572868
  95.4 2.0 copy-start.8
  97.3 84.0 %all-reduce.9.cloned.1.call-start = ((), (), s32[]{:S(2)}) async-start(), calls=%async_computation.7 | async-start | bytes 1048576 | tf_op jit(solution)/shard_map/psum | solution.py:80
  183.9 0.8 copy-start.4
  189.2 13.0 %all-to-all-start.4 = ((bf16[8,1,64,128]{3,2,1,0:T(8,128)(2,1)}), bf16[8,1,64,128]{3,2,1,0:T(8,128)(2,1)}, u32[]{:S(2)}, u32[]{:S(2)}) async-start(bf16[8,1,64,128]{3,2,1,0:T(8,128)(2,1)} %fusion.27), calls=%async_computation.4 | async-start | bytes 262144 | tf_op jit(solution)/shard_map/all_to_all | solution.py:70
  194.7 42.4 %all-reduce.11.cloned.1.call-start = ((), (), s32[]{:S(2)}) async-start(), calls=%async_computation.8 | async-start | bytes 1048576 | tf_op jit(solution)/shard_map/psum | solution.py:80
  237.1 2.9 %copy-start.3 = (bf16[8,64,512]{2,0,1:T(8,128)(2,1)S(1)}, bf16[8,64,512]{2,0,1:T(8,128)(2,1)}, u32[]{:S(2)}) copy-start(bf16[8,64,512]{2,0,1:T(8,128)(2,1)} %copy-done.2) | copy-start | bytes 1572868
  237.1 2.9 %copy-start.5 = (bf16[8,64,512]{2,0,1:T(8,128)(2,1)S(1)}, bf16[8,64,512]{2,0,1:T(8,128)(2,1)}, u32[]{:S(2)}) copy-start(bf16[8,64,512]{2,0,1:T(8,128)(2,1)} %copy-done.4) | copy-start | bytes 1572868
  241.6 1.4 copy-start.6
  241.6 1.4 copy-start.10
Sparse Core Ops, SparseCore 0:
  44.9 33.4 all-reduce.4
  97.4 30.0 all-reduce.6
  151.2 30.0 all-reduce.8
  207.0 30.0 all-reduce.10
where the time goes:
time: 252 us; the launch traced here: 251 us
  waiting for transfers between devices  128 us (51%)
  blocking collectives  39.6 us (16%)
  other arithmetic  20.7 us (8%)
  starting transfers between devices  19.1 us (8%)
  local copies, waits for them, and re-layouts  17.8 us (7%)
  between operations  14.8 us (6%)
  matrix products  10.1 us (4%)
    psum x4, waiting for transfers between devices, body(): lax.psum(partial_value.astype(jnp.bfloat16), 'blk').astype(jnp.float32)  121 us
    all_to_all x2, blocking collectives, body(): lax.all_to_all(outbound_rates, 'area', split_axis=0, concat_axis=0, tiled...  25.4 us
    all_to_all x2, starting transfers between devices, body(): lax.all_to_all(outbound_rates, 'area', split_axis=0, concat_axis=0, tiled...  11.5 us
    all_to_all x1, starting transfers between devices, body(): lax.all_to_all(request_table, 'area', split_axis=0, concat_axis=0, tiled=...  7.28 us
    all_gather x1, blocking collectives, body(): lax.all_gather(activity.astype(jnp.bfloat16), 'blk', axis=1, tiled=True)  7.17 us
    convert_element_type x4, other arithmetic, body(): rate_full = jnp.tanh(current).astype(jnp.bfloat16)  7.12 us
    all_gather x1, blocking collectives, body(): lax.all_gather(ext_input.astype(jnp.float32).astype(jnp.bfloat16), 'blk',...  7.01 us
    all_to_all x2, waiting for transfers between devices, body(): lax.all_to_all(outbound_rates, 'area', split_axis=0, concat_axis=0, tiled...  6.9 us
  transfers between devices with their start and end apart: 7, of which 6 were waited for; matrix products, arithmetic and copies ran while one was open for 2% of the time, Pallas kernels for 0%

commit v1 on v0

v1 whole, which is shorter than its diff:
```python
import functools

import jax
import jax.numpy as jnp
from jax import lax
from jax.experimental import pallas as pl
from jax.experimental.pallas import tpu as pltpu
from jax.sharding import PartitionSpec as P

STEPS = 4
EULER = 0.5
MESH = pl.DeviceIdType.MESH


def kernel(
    n_area,
    n_blk,
    dst_ref,
    src_ref,
    count_ref,
    hebb_ref,
    act_ref,
    ext_ref,
    w_ref,
    out_act,
    out_pl,
    act,
    rate_send,
    rate_recv,
    w_full,
    req_send,
    req_recv,
    post,
    pre,
    acc,
    req_ss,
    req_rs,
    w_ss,
    w_rs,
    r_ss,
    r_rs,
    p_ss,
    p_rs,
):
    n_sub, trials, quarter = act_ref.shape
    slots = w_ref.shape[0]
    a = lax.axis_index("area")
    b = lax.axis_index("blk")
    half = n_area // 2
    readers = (lax.rem(a + 1, n_area), lax.rem(a + n_area - 1, n_area), lax.rem(a + half, n_area))
    owners = (lax.rem(a + n_area - 1, n_area), lax.rem(a + 1, n_area), lax.rem(a + half, n_area))
    sibs = [lax.rem(b + s, n_blk) for s in range(1, n_blk)]
    order = (2, 0, 1)

    barrier = pltpu.get_barrier_semaphore()
    for k in range(slots):
        for s in range(n_blk):
            pl.semaphore_signal(
                barrier, inc=1, device_id=(readers[k], lax.rem(b + s, n_blk)), device_id_type=MESH
            )
    for s in sibs:
        pl.semaphore_signal(barrier, inc=1, device_id=(a, s), device_id_type=MESH)
    for k in range(slots):
        req_send[k] = jnp.full(req_send.shape[1:], lax.rem(src_ref[k], n_sub), jnp.int32)
    pl.semaphore_wait(barrier, slots * n_blk + n_blk - 1)

    pending = []
    req = []
    for k in order:
        c = pltpu.make_async_remote_copy(
            src_ref=req_send.at[k],
            dst_ref=req_recv.at[k],
            send_sem=req_ss.at[k],
            recv_sem=req_rs.at[k],
            device_id=(owners[k], b),
            device_id_type=MESH,
        )
        c.start()
        req.append(c)
        pending.append(c)

    def part(index):
        return pl.ds(pl.multiple_of(index * quarter, quarter), quarter)

    w_copies = []
    for n, s in enumerate(sibs):
        c = pltpu.make_async_remote_copy(
            src_ref=w_ref.at[:, :, part(s)],
            dst_ref=w_full.at[:, part(b), :],
            send_sem=w_ss.at[n],
            recv_sem=w_rs.at[n],
            device_id=(a, s),
            device_id_type=MESH,
        )
        c.start()
        w_copies.append(c)
        pending.append(c)

    act[...] = act_ref[...]
    for k in range(slots):
        w_full[k, part(b), :] = w_ref[k, :, part(b)]
    dst = [dst_ref[k] for k in range(slots)]
    occ = [(k < count_ref[0]).astype(jnp.float32) for k in range(slots)]

    for c in req:
        c.wait_recv()
    want = [jnp.max(req_recv[k]) for k in range(slots)]

    def center(x):
        x = x.astype(jnp.float32)
        return (x - jnp.mean(x, axis=0, keepdims=True)).astype(jnp.bfloat16)

    def updated(index, contrib):
        total = ext_ref[index].astype(jnp.float32)
        for k in range(slots):
            gate = (dst[k] == index).astype(jnp.float32) * occ[k]
            total = total + contrib[k] * gate
        now = act[index]
        return now + EULER * (total - now)

    def send_rates(t, rates):
        for k in order:
            rate_send[t, k] = rates[k]
            for s in range(n_blk):
                c = pltpu.make_async_remote_copy(
                    src_ref=rate_send.at[t, k],
                    dst_ref=rate_recv.at[t, k, b],
                    send_sem=r_ss.at[t, k, s],
                    recv_sem=r_rs.at[t, k],
                    device_id=(readers[k], lax.rem(b + s, n_blk)),
                    device_id_type=MESH,
                )
                c.start()
                pending.append(c)

    send_rates(0, [jnp.tanh(act[want[k]]).astype(jnp.bfloat16) for k in range(slots)])
    for c in w_copies:
        c.wait_recv()

    posts = []
    for t in range(STEPS):
        contrib = [None] * slots
        for k in (0, 1, 2):
            pltpu.make_async_copy(rate_recv.at[t, k], rate_recv.at[t, k], r_rs.at[t, k]).wait()
            rates = jnp.concatenate([rate_recv[t, k, j] for j in range(n_blk)], axis=1)
            contrib[k] = jnp.dot(rates, w_full[k], preferred_element_type=jnp.float32)
        if t < STEPS - 1:
            send_rates(
                t + 1,
                [jnp.tanh(updated(want[k], contrib)).astype(jnp.bfloat16) for k in range(slots)],
            )
        for k in range(slots):
            post[t, b, k] = center(jnp.tanh(updated(dst[k], contrib)).astype(jnp.bfloat16))
        step_posts = []
        for n, s in enumerate(sibs):
            c = pltpu.make_async_remote_copy(
                src_ref=post.at[t, b],
                dst_ref=post.at[t, b],
                send_sem=p_ss.at[t, n],
                recv_sem=p_rs.at[t, n],
                device_id=(a, s),
                device_id_type=MESH,
            )
            c.start()
            step_posts.append(c)
            pending.append(c)
        posts.append(step_posts)
        for d in range(n_sub):
            value = updated(d, contrib)
            if t < STEPS - 1:
                act[d] = value
            else:
                out_act[d] = value
        for k in range(slots):
            pre[k, pl.ds(t * trials, trials), :] = center(rate_recv[t, k, b])

    def change(k, first, last):
        x = pre[k, first * trials : last * trials, :]
        y = jnp.concatenate(
            [
                post[first:last, j, k].reshape((last - first) * trials, quarter)
                for j in range(n_blk)
            ],
            axis=1,
        )
        return lax.dot_general(
            x, y, (((0,), (0,)), ((), ())), preferred_element_type=jnp.float32
        )

    for t in range(STEPS - 1):
        for c in posts[t]:
            c.wait_recv()
    for k in range(slots):
        acc[k] = change(k, 0, STEPS - 1)
    for c in posts[STEPS - 1]:
        c.wait_recv()
    scale = (STEPS * trials) ** -0.5
    for k in range(slots):
        gate = occ[k] * (hebb_ref[k] == 1).astype(jnp.float32) * scale
        out_pl[k] = ((acc[k] + change(k, STEPS - 1, STEPS)) * gate).astype(jnp.bfloat16)
    for c in pending:
        c.wait_send()


def body(n_area, n_blk, activity, ext_input, weights, slot_dst, slot_src, slot_count, hebb_mask):
    n_sub, _, trials, quarter = activity.shape
    slots, _, _, width = weights.shape
    vmem = pl.BlockSpec(memory_space=pltpu.VMEM)
    smem = pl.BlockSpec(memory_space=pltpu.SMEM)
    bf16 = jnp.bfloat16
    dma = pltpu.SemaphoreType.DMA
    act, plast = pl.pallas_call(
        functools.partial(kernel, n_area, n_blk),
        out_shape=(
            jax.ShapeDtypeStruct((n_sub, trials, quarter), jnp.float32),
            jax.ShapeDtypeStruct((slots, quarter, width), bf16),
        ),
        in_specs=[smem] * 4 + [vmem] * 3,
        out_specs=(vmem, vmem),
        scratch_shapes=[
            pltpu.VMEM((n_sub, trials, quarter), jnp.float32),
            pltpu.VMEM((STEPS, slots, trials, quarter), bf16),
            pltpu.VMEM((STEPS, slots, n_blk, trials, quarter), bf16),
            pltpu.VMEM((slots, width, quarter), bf16),
            pltpu.VMEM((slots, 8, 128), jnp.int32),
            pltpu.VMEM((slots, 8, 128), jnp.int32),
            pltpu.VMEM((STEPS, n_blk, slots, trials, quarter), bf16),
            pltpu.VMEM((slots, STEPS * trials, quarter), bf16),
            pltpu.VMEM((slots, quarter, width), jnp.float32),
            dma((slots,)),
            dma((slots,)),
            dma((n_blk - 1,)),
            dma((n_blk - 1,)),
            dma((STEPS, slots, n_blk)),
            dma((STEPS, slots)),
            dma((STEPS, n_blk - 1)),
            dma((STEPS, n_blk - 1)),
        ],
        compiler_params=pltpu.CompilerParams(
            collective_id=0, has_side_effects=True, vmem_limit_bytes=24 * 1024 * 1024
        ),
    )(
        slot_dst,
        slot_src,
        slot_count,
        hebb_mask,
        activity.reshape(n_sub, trials, quarter),
        ext_input.reshape(n_sub, trials, quarter),
        weights.reshape(slots, quarter, width),
    )
    return act[:, None], plast[:, None]


def solution(mesh):
    p4 = P("area", "blk", None, None)
    p1 = P("area")
    return jax.shard_map(
        functools.partial(body, mesh.shape["area"], mesh.shape["blk"]),
        mesh=mesh,
        in_specs=(p4, p4, p4, p1, p1, p1, p1),
        out_specs=(p4, p4),
        check_vma=False,
    )
```

time: 252 us -> 47.5 us (0.19)
  waiting for transfers between devices: 128 us -> 0 us
  Pallas kernels: 0 us -> 41 us
  blocking collectives: 39.6 us -> 0 us
  other arithmetic: 20.7 us -> 0 us
  starting transfers between devices: 19.1 us -> 0 us
  between operations: 14.8 us -> 1.32 us
  local copies, waits for them, and re-layouts: 17.8 us -> 4.96 us
  matrix products: 10.1 us -> 0 us
    psum x4 -> x0, waiting for transfers between devices: 121 us -> none  [body(): lax.psum(partial_value.astype(jnp.bfloat16), 'blk').astype(jnp.float32)]
    pallas_call x0 -> x1, Pallas kernels: none -> 41 us  [body(): pl.pallas_call(functools.partial(kernel, n_area, n_blk), out_shape=(jax.S...]
    all_to_all x2 -> x0, blocking collectives: 25.4 us -> none  [body(): lax.all_to_all(outbound_rates, 'area', split_axis=0, concat_axis=0, tiled...]
    all_to_all x3 -> x0, starting transfers between devices: 18.8 us -> none  [the longest x2 11.5 us: body(): lax.all_to_all(outbound_rates, 'area', split_axis=0, concat_axis=0, tiled...]
    all_gather x2 -> x0, blocking collectives: 14.2 us -> none  [the longest x1 7.17 us: body(): lax.all_gather(activity.astype(jnp.bfloat16), 'blk', axis=1, tiled=True)]
    gather x9 -> x0, local copies, waits for them, and re-layouts: 11.3 us -> none  [the longest x4 5.39 us: body(): rates_own[pick_idx]]
    convert_element_type x8 -> x0, other arithmetic: 10.7 us -> none  [the longest x4 7.12 us: body(): rate_full = jnp.tanh(current).astype(jnp.bfloat16)]
    dot_general x9 -> x0, matrix products: 10.1 us -> none  [the longest x4 6.72 us: body(): jnp.einsum('kd,kts->dts', select, input_contribution, precision=lax.Preci...]
  transfers between devices with their start and end apart: 7 -> 0, of which waited for: 6 -> 0; matrix products, arithmetic and copies ran while one was open for 2% -> 0% of each run, Pallas kernels for 0% -> 0%
where the time goes in v1:
time: 47.5 us; the launch traced here: 47.2 us
  Pallas kernels  41 us (86%)
  local copies, waits for them, and re-layouts  4.96 us (10%)
  between operations  1.32 us (3%)
    pallas_call x1, Pallas kernels, body(): pl.pallas_call(functools.partial(kernel, n_area, n_blk), out_shape=(jax.S...  41 us
    unnamed x14, local copies, waits for them, and re-layouts  4.96 us

profile of v1, /device:TPU:0, one launch (start us, length us, event | category | flops | bytes accessed | tf_op | source)
XLA Modules:
  0.0 47.2 jit_solution(12868526553152154475)
XLA Ops:
  1.3 0.0 copy-start.3
  1.3 0.0 copy-start.4
  1.3 0.0 copy-start.5
  1.3 0.6 %copy-done.3 = s32[3]{0:T(128)S(1)} copy-done((s32[3]{0:T(128)S(1)}, s32[3]{0:T(128)}, u32[]{:S(2)}) %copy-start.3) | copy-done | bytes 36
  1.9 0.0 copy-done.4
  2.0 0.0 copy-done.5
  2.0 0.0 copy-start
  2.0 1.0 %copy-done = bf16[3,1,128,512]{3,2,1,0:T(8,128)(2,1)S(1)} copy-done((bf16[3,1,128,512]{3,2,1,0:T(8,128)(2,1)S(1)}, bf16[3,1,128,512]{3,2,1,0:T(8,128)(2,1)}, u32[]{:S(2)}) %copy-start) | copy-done | bytes 393240
  3.0 0.0 copy-start.1
  3.0 0.9 %copy-done.1 = f32[8,1,64,128]{3,2,1,0:T(8,128)S(1)} copy-done((f32[8,1,64,128]{3,2,1,0:T(8,128)S(1)}, f32[8,1,64,128]{3,2,1,0:T(8,128)}, u32[]{:S(2)}) %copy-start.1) | copy-done | bytes 262168
  3.9 0.0 copy-start.2
  3.9 0.9 %copy-done.2 = bf16[8,1,64,128]{3,2,1,0:T(8,128)(2,1)S(1)} copy-done((bf16[8,1,64,128]{3,2,1,0:T(8,128)(2,1)S(1)}, bf16[8,1,64,128]{3,2,1,0:T(8,128)(2,1)}, u32[]{:S(2)}) %copy-start.2) | copy-done | bytes 131096
  4.8 41.0 %shard_map.86 = (f32[8,64,128]{2,1,0:T(8,128)S(1)}, bf16[3,128,512]{2,1,0:T(8,128)(2,1)S(1)}) custom-call(s32[3]{0:T(128)S(1)} %copy-done.3, s32[3]{0:T(128)S(1)} %copy-done.4, s32[1]{0:T(128)S(6)} %copy.13.count_ref, s32[3]{0:T(128)S(1)} %copy-done.5, f32[8,64,128]{2,1,0:T(8,128)S(1)} %bitcast.11, bf16[8,64,128]{2,1,0:T(8,128)(2,1)S(1)} %bitcast.13, ...), custom_call_target="tpu_custom_call" | custom-call | tf_op jit(solution)/shard_map/pallas_call | solution.py:212
  45.8 0.7 %copy.14 = f32[8,1,64,128]{3,2,1,0:T(8,128)} copy(f32[8,1,64,128]{3,2,1,0:T(8,128)S(1)} %bitcast.12) | data formatting | bytes 524288
  46.5 0.7 %copy.15 = bf16[3,1,128,512]{3,2,1,0:T(8,128)(2,1)} copy(bf16[3,1,128,512]{3,2,1,0:T(8,128)(2,1)S(1)} %bitcast.10) | data formatting | bytes 786432
Async XLA Ops:
  1.3 0.7 %copy-start.3 = (s32[3]{0:T(128)S(1)}, s32[3]{0:T(128)}, u32[]{:S(2)}) copy-start(s32[3]{0:T(128)} %dst_ref.1) | copy-start | bytes 40
  1.3 0.7 %copy-start.4 = (s32[3]{0:T(128)S(1)}, s32[3]{0:T(128)}, u32[]{:S(2)}) copy-start(s32[3]{0:T(128)} %src_ref.1) | copy-start | bytes 40
  1.3 0.7 %copy-start.5 = (s32[3]{0:T(128)S(1)}, s32[3]{0:T(128)}, u32[]{:S(2)}) copy-start(s32[3]{0:T(128)} %hebb_ref.1) | copy-start | bytes 40
  2.0 1.0 %copy-start = (bf16[3,1,128,512]{3,2,1,0:T(8,128)(2,1)S(1)}, bf16[3,1,128,512]{3,2,1,0:T(8,128)(2,1)}, u32[]{:S(2)}) copy-start(bf16[3,1,128,512]{3,2,1,0:T(8,128)(2,1)} %param.9) | copy-start | bytes 1179652
  3.0 0.9 %copy-start.1 = (f32[8,1,64,128]{3,2,1,0:T(8,128)S(1)}, f32[8,1,64,128]{3,2,1,0:T(8,128)}, u32[]{:S(2)}) copy-start(f32[8,1,64,128]{3,2,1,0:T(8,128)} %param.7) | copy-start | bytes 786436
  3.9 0.9 %copy-start.2 = (bf16[8,1,64,128]{3,2,1,0:T(8,128)(2,1)S(1)}, bf16[8,1,64,128]{3,2,1,0:T(8,128)(2,1)}, u32[]{:S(2)}) copy-start(bf16[8,1,64,128]{3,2,1,0:T(8,128)(2,1)} %param.8) | copy-start | bytes 393220

commit v2 on v1

--- a/solution.py
+++ b/solution.py
@@ -15,16 +15,21 @@
 def kernel(
     n_area,
     n_blk,
+    dst_hbm,
+    src_hbm,
+    count_hbm,
+    hebb_hbm,
+    act_hbm,
+    ext_hbm,
+    w_ref,
+    out_act,
+    out_pl,
     dst_ref,
     src_ref,
     count_ref,
     hebb_ref,
-    act_ref,
+    act,
     ext_ref,
-    w_ref,
-    out_act,
-    out_pl,
-    act,
     rate_send,
     rate_recv,
     w_full,
@@ -41,8 +46,9 @@
     r_rs,
     p_ss,
     p_rs,
+    in_sem,
 ):
-    n_sub, trials, quarter = act_ref.shape
+    n_sub, trials, quarter = act.shape
     slots = w_ref.shape[0]
     a = lax.axis_index("area")
     b = lax.axis_index("blk")
@@ -50,7 +56,27 @@
     readers = (lax.rem(a + 1, n_area), lax.rem(a + n_area - 1, n_area), lax.rem(a + half, n_area))
     owners = (lax.rem(a + n_area - 1, n_area), lax.rem(a + 1, n_area), lax.rem(a + half, n_area))
     sibs = [lax.rem(b + s, n_blk) for s in range(1, n_blk)]
-    order = (2, 0, 1)
+    order = (0, 1, 2)
+
+    def part(index):
+        return pl.ds(pl.multiple_of(index * quarter, quarter), quarter)
+
+    loads = [
+        pltpu.make_async_copy(x, y, in_sem.at[n])
+        for n, (x, y) in enumerate(
+            (
+                (src_hbm, src_ref),
+                (dst_hbm, dst_ref),
+                (count_hbm, count_ref),
+                (hebb_hbm, hebb_ref),
+                (act_hbm, act),
+                (ext_hbm, ext_ref),
+                (w_ref.at[:, :, part(b)], w_full.at[:, part(b), :]),
+            )
+        )
+    ]
+    for c in loads:
+        c.start()
 
     barrier = pltpu.get_barrier_semaphore()
     for k in range(slots):
@@ -60,6 +86,7 @@
             )
     for s in sibs:
         pl.semaphore_signal(barrier, inc=1, device_id=(a, s), device_id_type=MESH)
+    loads[0].wait()
     for k in range(slots):
         req_send[k] = jnp.full(req_send.shape[1:], lax.rem(src_ref[k], n_sub), jnp.int32)
     pl.semaphore_wait(barrier, slots * n_blk + n_blk - 1)
@@ -79,9 +106,6 @@
         req.append(c)
         pending.append(c)
 
-    def part(index):
-        return pl.ds(pl.multiple_of(index * quarter, quarter), quarter)
-
     w_copies = []
     for n, s in enumerate(sibs):
         c = pltpu.make_async_remote_copy(
@@ -96,9 +120,8 @@
         w_copies.append(c)
         pending.append(c)
 
-    act[...] = act_ref[...]
-    for k in range(slots):
-        w_full[k, part(b), :] = w_ref[k, :, part(b)]
+    for c in loads[1:]:
+        c.wait()
     dst = [dst_ref[k] for k in range(slots)]
     occ = [(k < count_ref[0]).astype(jnp.float32) for k in range(slots)]
 
@@ -206,7 +229,7 @@
     n_sub, _, trials, quarter = activity.shape
     slots, _, _, width = weights.shape
     vmem = pl.BlockSpec(memory_space=pltpu.VMEM)
-    smem = pl.BlockSpec(memory_space=pltpu.SMEM)
+    hbm = pl.BlockSpec(memory_space=pltpu.HBM)
     bf16 = jnp.bfloat16
     dma = pltpu.SemaphoreType.DMA
     act, plast = pl.pallas_call(
@@ -215,10 +238,15 @@
             jax.ShapeDtypeStruct((n_sub, trials, quarter), jnp.float32),
             jax.ShapeDtypeStruct((slots, quarter, width), bf16),
         ),
-        in_specs=[smem] * 4 + [vmem] * 3,
+        in_specs=[hbm] * 7,
         out_specs=(vmem, vmem),
         scratch_shapes=[
+            pltpu.SMEM((slots,), jnp.int32),
+            pltpu.SMEM((slots,), jnp.int32),
+            pltpu.SMEM((1,), jnp.int32),
+            pltpu.SMEM((slots,), jnp.int32),
             pltpu.VMEM((n_sub, trials, quarter), jnp.float32),
+            pltpu.VMEM((n_sub, trials, quarter), bf16),
             pltpu.VMEM((STEPS, slots, trials, quarter), bf16),
             pltpu.VMEM((STEPS, slots, n_blk, trials, quarter), bf16),
             pltpu.VMEM((slots, width, quarter), bf16),
@@ -235,6 +263,7 @@
             dma((STEPS, slots)),
             dma((STEPS, n_blk - 1)),
             dma((STEPS, n_blk - 1)),
+            dma((7,)),
         ],
         compiler_params=pltpu.CompilerParams(
             collective_id=0, has_side_effects=True, vmem_limit_bytes=24 * 1024 * 1024

time: 47.5 us -> 44 us (0.926)
  Pallas kernels: 41 us -> 37.4 us
    pallas_call x1, Pallas kernels: 41 us -> 37.4 us  [body(): pl.pallas_call(functools.partial(kernel, n_area, n_blk), out_shape=(jax.S...]
where the time goes in v2:
time: 44 us; the launch traced here: 43.7 us
  Pallas kernels  37.4 us (85%)
  local copies, waits for them, and re-layouts  4.96 us (11%)
  between operations  1.32 us (3%)
    pallas_call x1, Pallas kernels, body(): pl.pallas_call(functools.partial(kernel, n_area, n_blk), out_shape=(jax.S...  37.4 us
    unnamed x14, local copies, waits for them, and re-layouts  4.96 us

profile of v2, /device:TPU:0, one launch (start us, length us, event | category | flops | bytes accessed | tf_op | source)
XLA Modules:
  0.0 43.7 jit_solution(5109922527772928972)
XLA Ops:
  1.3 0.0 copy-start.3
  1.3 0.0 copy-start.4
  1.3 0.0 copy-start.5
  1.3 0.6 %copy-done.3 = s32[3]{0:T(128)S(1)} copy-done((s32[3]{0:T(128)S(1)}, s32[3]{0:T(128)}, u32[]{:S(2)}) %copy-start.3) | copy-done | bytes 36
  1.9 0.0 copy-done.4
  2.0 0.0 copy-done.5
  2.0 0.0 copy-start
  2.0 1.0 %copy-done = bf16[3,1,128,512]{3,2,1,0:T(8,128)(2,1)S(1)} copy-done((bf16[3,1,128,512]{3,2,1,0:T(8,128)(2,1)S(1)}, bf16[3,1,128,512]{3,2,1,0:T(8,128)(2,1)}, u32[]{:S(2)}) %copy-start) | copy-done | bytes 393240
  3.0 0.0 copy-start.1
  3.0 0.9 %copy-done.1 = f32[8,1,64,128]{3,2,1,0:T(8,128)S(1)} copy-done((f32[8,1,64,128]{3,2,1,0:T(8,128)S(1)}, f32[8,1,64,128]{3,2,1,0:T(8,128)}, u32[]{:S(2)}) %copy-start.1) | copy-done | bytes 262168
  3.9 0.0 copy-start.2
  3.9 0.9 %copy-done.2 = bf16[8,1,64,128]{3,2,1,0:T(8,128)(2,1)S(1)} copy-done((bf16[8,1,64,128]{3,2,1,0:T(8,128)(2,1)S(1)}, bf16[8,1,64,128]{3,2,1,0:T(8,128)(2,1)}, u32[]{:S(2)}) %copy-start.2) | copy-done | bytes 131096
  4.8 37.4 %shard_map.86 = (f32[8,64,128]{2,1,0:T(8,128)S(1)}, bf16[3,128,512]{2,1,0:T(8,128)(2,1)S(1)}) custom-call(s32[3]{0:T(128)S(1)} %copy-done.3, s32[3]{0:T(128)S(1)} %copy-done.4, s32[1]{0:T(128)S(6)} %copy.13.count_hbm, s32[3]{0:T(128)S(1)} %copy-done.5, f32[8,64,128]{2,1,0:T(8,128)S(1)} %bitcast.11, bf16[8,64,128]{2,1,0:T(8,128)(2,1)S(1)} %bitcast.13, ...), custom_call_target="tpu_custom_call" | custom-call | tf_op jit(solution)/shard_map/pallas_call | solution.py:235
  42.2 0.7 %copy.14 = f32[8,1,64,128]{3,2,1,0:T(8,128)} copy(f32[8,1,64,128]{3,2,1,0:T(8,128)S(1)} %bitcast.12) | data formatting | bytes 524288
  42.9 0.7 %copy.15 = bf16[3,1,128,512]{3,2,1,0:T(8,128)(2,1)} copy(bf16[3,1,128,512]{3,2,1,0:T(8,128)(2,1)S(1)} %bitcast.10) | data formatting | bytes 786432
Async XLA Ops:
  1.3 0.7 %copy-start.3 = (s32[3]{0:T(128)S(1)}, s32[3]{0:T(128)}, u32[]{:S(2)}) copy-start(s32[3]{0:T(128)} %dst_hbm.1) | copy-start | bytes 40
  1.3 0.7 %copy-start.4 = (s32[3]{0:T(128)S(1)}, s32[3]{0:T(128)}, u32[]{:S(2)}) copy-start(s32[3]{0:T(128)} %src_hbm.1) | copy-start | bytes 40
  1.3 0.7 %copy-start.5 = (s32[3]{0:T(128)S(1)}, s32[3]{0:T(128)}, u32[]{:S(2)}) copy-start(s32[3]{0:T(128)} %hebb_hbm.1) | copy-start | bytes 40
  2.0 1.0 %copy-start = (bf16[3,1,128,512]{3,2,1,0:T(8,128)(2,1)S(1)}, bf16[3,1,128,512]{3,2,1,0:T(8,128)(2,1)}, u32[]{:S(2)}) copy-start(bf16[3,1,128,512]{3,2,1,0:T(8,128)(2,1)} %param.9) | copy-start | bytes 1179652
  3.0 0.9 %copy-start.1 = (f32[8,1,64,128]{3,2,1,0:T(8,128)S(1)}, f32[8,1,64,128]{3,2,1,0:T(8,128)}, u32[]{:S(2)}) copy-start(f32[8,1,64,128]{3,2,1,0:T(8,128)} %param.7) | copy-start | bytes 786436
  3.9 0.9 %copy-start.2 = (bf16[8,1,64,128]{3,2,1,0:T(8,128)(2,1)S(1)}, bf16[8,1,64,128]{3,2,1,0:T(8,128)(2,1)}, u32[]{:S(2)}) copy-start(bf16[8,1,64,128]{3,2,1,0:T(8,128)(2,1)} %param.8) | copy-start | bytes 393220

commit v3 on v2

--- a/solution.py
+++ b/solution.py
@@ -47,6 +47,7 @@
     p_ss,
     p_rs,
     in_sem,
+    plast,
 ):
     n_sub, trials, quarter = act.shape
     slots = w_ref.shape[0]
@@ -55,8 +56,10 @@
     half = n_area // 2
     readers = (lax.rem(a + 1, n_area), lax.rem(a + n_area - 1, n_area), lax.rem(a + half, n_area))
     owners = (lax.rem(a + n_area - 1, n_area), lax.rem(a + 1, n_area), lax.rem(a + half, n_area))
-    sibs = [lax.rem(b + s, n_blk) for s in range(1, n_blk)]
+    shifts = [n_blk // 2] + [s for s in range(1, n_blk) if s != n_blk // 2]
+    sibs = [lax.rem(b + s, n_blk) for s in shifts]
     order = (0, 1, 2)
+    sends = [(k, s) for k in order for s in (2, 3, 0, 1)[:n_blk]]
 
     def part(index):
         return pl.ds(pl.multiple_of(index * quarter, quarter), quarter)
@@ -144,7 +147,8 @@
     def send_rates(t, rates):
         for k in order:
             rate_send[t, k] = rates[k]
-            for s in range(n_blk):
+        for k, s in sends:
+            if True:
                 c = pltpu.make_async_remote_copy(
                     src_ref=rate_send.at[t, k],
                     dst_ref=rate_recv.at[t, k, b],
@@ -161,6 +165,7 @@
         c.wait_recv()
 
     posts = []
+    stores = []
     for t in range(STEPS):
         contrib = [None] * slots
         for k in (0, 1, 2):
@@ -190,10 +195,10 @@
         posts.append(step_posts)
         for d in range(n_sub):
             value = updated(d, contrib)
-            if t < STEPS - 1:
-                act[d] = value
-            else:
-                out_act[d] = value
+            act[d] = value
+        if t == STEPS - 1:
+            stores.append(pltpu.make_async_copy(act, out_act, in_sem.at[0]))
+            stores[-1].start()
         for k in range(slots):
             pre[k, pl.ds(t * trials, trials), :] = center(rate_recv[t, k, b])
 
@@ -220,7 +225,11 @@
     scale = (STEPS * trials) ** -0.5
     for k in range(slots):
         gate = occ[k] * (hebb_ref[k] == 1).astype(jnp.float32) * scale
-        out_pl[k] = ((acc[k] + change(k, STEPS - 1, STEPS)) * gate).astype(jnp.bfloat16)
+        plast[k] = ((acc[k] + change(k, STEPS - 1, STEPS)) * gate).astype(jnp.bfloat16)
+        stores.append(pltpu.make_async_copy(plast.at[k], out_pl.at[k], in_sem.at[k + 1]))
+        stores[-1].start()
+    for c in stores:
+        c.wait()
     for c in pending:
         c.wait_send()
 
@@ -228,8 +237,7 @@
 def body(n_area, n_blk, activity, ext_input, weights, slot_dst, slot_src, slot_count, hebb_mask):
     n_sub, _, trials, quarter = activity.shape
     slots, _, _, width = weights.shape
-    vmem = pl.BlockSpec(memory_space=pltpu.VMEM)
-    hbm = pl.BlockSpec(memory_space=pltpu.HBM)
+    hbm = pl.BlockSpec(memory_space=pl.ANY)
     bf16 = jnp.bfloat16
     dma = pltpu.SemaphoreType.DMA
     act, plast = pl.pallas_call(
@@ -239,7 +247,7 @@
             jax.ShapeDtypeStruct((slots, quarter, width), bf16),
         ),
         in_specs=[hbm] * 7,
-        out_specs=(vmem, vmem),
+        out_specs=(hbm, hbm),
         scratch_shapes=[
             pltpu.SMEM((slots,), jnp.int32),
             pltpu.SMEM((slots,), jnp.int32),
@@ -264,9 +272,10 @@
             dma((STEPS, n_blk - 1)),
             dma((STEPS, n_blk - 1)),
             dma((7,)),
+            pltpu.VMEM((slots, quarter, width), bf16),
         ],
         compiler_params=pltpu.CompilerParams(
-            collective_id=0, has_side_effects=True, vmem_limit_bytes=24 * 1024 * 1024
+            collective_id=0, has_side_effects=True, vmem_limit_bytes=62 * 1024 * 1024
         ),
     )(
         slot_dst,

time: 44 us -> 41.4 us (0.941)
  local copies, waits for them, and re-layouts: 4.96 us -> 2.47 us
    unnamed x14 -> x4, local copies, waits for them, and re-layouts: 4.96 us -> 2.47 us
where the time goes in v3:
time: 41.4 us; the launch traced here: 41.1 us
  Pallas kernels  37.3 us (90%)
  local copies, waits for them, and re-layouts  2.47 us (6%)
  between operations  1.29 us (3%)
    pallas_call x1, Pallas kernels, body(): pl.pallas_call(functools.partial(kernel, n_area, n_blk), out_shape=(jax.S...  37.3 us
    unnamed x4, local copies, waits for them, and re-layouts  2.47 us

profile of v3, /device:TPU:0, one launch (start us, length us, event | category | flops | bytes accessed | tf_op | source)
XLA Modules:
  0.0 41.1 jit_solution(4177138571844131830)
XLA Ops:
  1.3 37.3 %shard_map.86 = (f32[8,64,128]{2,1,0:T(8,128)}, bf16[3,128,512]{2,1,0:T(8,128)(2,1)}) custom-call(s32[3]{0:T(128)} %dst_hbm.1, s32[3]{0:T(128)} %src_hbm.1, s32[1]{0:T(128)S(6)} %copy.13.count_hbm, s32[3]{0:T(128)} %hebb_hbm.1, f32[8,64,128]{2,1,0:T(8,128)} %bitcast.11, bf16[8,64,128]{2,1,0:T(8,128)(2,1)} %bitcast.13, bf16[3,128,512]{2,1,0:T(8,128)(2,1)} %bitcast.9), custom_call_target="tpu_custom_call" | custom-call | tf_op jit(solution)/shard_map/pallas_call | solution.py:243
  38.6 0.0 copy-start
  38.6 1.7 %copy.14 = f32[8,1,64,128]{3,2,1,0:T(8,128)} copy(f32[8,1,64,128]{3,2,1,0:T(8,128)} %bitcast.12) | data formatting | bytes 524288
  40.4 0.0 copy-done
  40.4 0.7 %copy.15 = bf16[3,1,128,512]{3,2,1,0:T(8,128)(2,1)} copy(bf16[3,1,128,512]{3,2,1,0:T(8,128)(2,1)S(1)} %bitcast.10) | data formatting | bytes 786432
Async XLA Ops:
  38.6 1.7 %copy-start = (bf16[3,128,512]{2,1,0:T(8,128)(2,1)S(1)}, bf16[3,128,512]{2,1,0:T(8,128)(2,1)}, u32[]{:S(2)}) copy-start(bf16[3,128,512]{2,1,0:T(8,128)(2,1)} %get-tuple-element.5) | copy-start | bytes 1179652

commit v4 on v3

--- a/solution.py
+++ b/solution.py
@@ -59,7 +59,12 @@
     shifts = [n_blk // 2] + [s for s in range(1, n_blk) if s != n_blk // 2]
     sibs = [lax.rem(b + s, n_blk) for s in shifts]
     order = (0, 1, 2)
-    sends = [(k, s) for k in order for s in (2, 3, 0, 1)[:n_blk]]
+    lead = 1 - lax.rem(a, 2)
+    near = 1 - lead
+    to_lead = lax.rem(a + 1 + lead * (n_area - 2), n_area)
+    to_near = lax.rem(a + 1 + near * (n_area - 2), n_area)
+    paths = ((lead, to_lead), (near, to_near), (2, readers[2]))
+    sends = [(k, to, s) for k, to in paths for s in (2, 3, 0, 1)[:n_blk]]
 
     def part(index):
         return pl.ds(pl.multiple_of(index * quarter, quarter), quarter)
@@ -147,14 +152,14 @@
     def send_rates(t, rates):
         for k in order:
             rate_send[t, k] = rates[k]
-        for k, s in sends:
+        for k, to, s in sends:
             if True:
                 c = pltpu.make_async_remote_copy(
                     src_ref=rate_send.at[t, k],
                     dst_ref=rate_recv.at[t, k, b],
                     send_sem=r_ss.at[t, k, s],
                     recv_sem=r_rs.at[t, k],
-                    device_id=(readers[k], lax.rem(b + s, n_blk)),
+                    device_id=(to, lax.rem(b + s, n_blk)),
                     device_id_type=MESH,
                 )
                 c.start()
@@ -164,7 +169,23 @@
     for c in w_copies:
         c.wait_recv()
 
-    posts = []
+    across = []
+    beside = []
+    mate = b + 1 - 2 * lax.rem(b, 2)
+
+    def post_copy(t, piece, to, n):
+        c = pltpu.make_async_remote_copy(
+            src_ref=post.at[t, piece],
+            dst_ref=post.at[t, piece],
+            send_sem=p_ss.at[t, n],
+            recv_sem=p_rs.at[t, n],
+            device_id=(a, to),
+            device_id_type=MESH,
+        )
+        c.start()
+        pending.append(c)
+        return c
+
     stores = []
     for t in range(STEPS):
         contrib = [None] * slots
@@ -179,20 +200,14 @@
             )
         for k in range(slots):
             post[t, b, k] = center(jnp.tanh(updated(dst[k], contrib)).astype(jnp.bfloat16))
-        step_posts = []
-        for n, s in enumerate(sibs):
-            c = pltpu.make_async_remote_copy(
-                src_ref=post.at[t, b],
-                dst_ref=post.at[t, b],
-                send_sem=p_ss.at[t, n],
-                recv_sem=p_rs.at[t, n],
-                device_id=(a, s),
-                device_id_type=MESH,
-            )
-            c.start()
-            step_posts.append(c)
-            pending.append(c)
-        posts.append(step_posts)
+        if t == STEPS - 1:
+            last_posts = [post_copy(t, b, s, n) for n, s in enumerate(sibs)]
+        else:
+            across.append(post_copy(t, b, sibs[0], 0))
+            beside.append(post_copy(t, b, mate, 1))
+        if t > 0:
+            across[t - 1].wait_recv()
+            beside.append(post_copy(t - 1, sibs[0], mate, 2))
         for d in range(n_sub):
             value = updated(d, contrib)
             act[d] = value
@@ -215,12 +230,11 @@
             x, y, (((0,), (0,)), ((), ())), preferred_element_type=jnp.float32
         )
 
-    for t in range(STEPS - 1):
-        for c in posts[t]:
-            c.wait_recv()
+    for c in beside:
+        c.wait_recv()
     for k in range(slots):
         acc[k] = change(k, 0, STEPS - 1)
-    for c in posts[STEPS - 1]:
+    for c in last_posts:
         c.wait_recv()
     scale = (STEPS * trials) ** -0.5
     for k in range(slots):

time: 41.4 us -> 41.4 us (level)
  no operation moved by 1% of the time
where the time goes in v4:
time: 41.4 us; the launch traced here: 41 us
  Pallas kernels  37.2 us (90%)
  local copies, waits for them, and re-layouts  2.47 us (6%)
  between operations  1.29 us (3%)
    pallas_call x1, Pallas kernels, body(): pl.pallas_call(functools.partial(kernel, n_area, n_blk), out_shape=(jax.S...  37.2 us
    unnamed x4, local copies, waits for them, and re-layouts  2.47 us

profile of v4, /device:TPU:0, one launch (start us, length us, event | category | flops | bytes accessed | tf_op | source)
XLA Modules:
  0.0 41.0 jit_solution(7580844201787192014)
XLA Ops:
  1.3 37.2 %shard_map.86 = (f32[8,64,128]{2,1,0:T(8,128)}, bf16[3,128,512]{2,1,0:T(8,128)(2,1)}) custom-call(s32[3]{0:T(128)} %dst_hbm.1, s32[3]{0:T(128)} %src_hbm.1, s32[1]{0:T(128)S(6)} %copy.13.count_hbm, s32[3]{0:T(128)} %hebb_hbm.1, f32[8,64,128]{2,1,0:T(8,128)} %bitcast.11, bf16[8,64,128]{2,1,0:T(8,128)(2,1)} %bitcast.13, bf16[3,128,512]{2,1,0:T(8,128)(2,1)} %bitcast.9), custom_call_target="tpu_custom_call" | custom-call | tf_op jit(solution)/shard_map/pallas_call | solution.py:257
  38.5 0.0 copy-start
  38.5 1.7 %copy.14 = f32[8,1,64,128]{3,2,1,0:T(8,128)} copy(f32[8,1,64,128]{3,2,1,0:T(8,128)} %bitcast.12) | data formatting | bytes 524288
  40.2 0.0 copy-done
  40.2 0.7 %copy.15 = bf16[3,1,128,512]{3,2,1,0:T(8,128)(2,1)} copy(bf16[3,1,128,512]{3,2,1,0:T(8,128)(2,1)S(1)} %bitcast.10) | data formatting | bytes 786432
Async XLA Ops:
  38.5 1.7 %copy-start = (bf16[3,128,512]{2,1,0:T(8,128)(2,1)S(1)}, bf16[3,128,512]{2,1,0:T(8,128)(2,1)}, u32[]{:S(2)}) copy-start(bf16[3,128,512]{2,1,0:T(8,128)(2,1)} %get-tuple-element.5) | copy-start | bytes 1179652
